TPU v7x, 256 devices: a whole 4x4x8 slice. The times are simulated.
256 devices in a mesh: row: 8 (over y_lo, x), col: 32 (over y_hi, z, core).
Axes of the slice: x: 4, y: 4 (y_hi: 2, y_lo: 2; y = y_hi * 2 + y_lo), z: 8, core: 2. Of those that a mesh axis runs over, the one named last changes fastest.
Arguments:
- p_blocks: bfloat16 [8, 3, 256, 128, 128], P('row', None, 'col'), may hold values from -1.1953125 to 1.1953125
- p_rows: int32 [8, 3, 256], P('row', None, 'col'), may hold values from -1 to 31, as said below
- c_rows: int32 [8, 3, 256], P('row', None, 'col'), may hold values from 0 to 31, as said below
Outputs:
- c_blocks: float32 [8, 3, 256, 128, 128], P('row', None, 'col')
Inputs may be any that keep to these rules, and one draw needn't show every extreme that they name: `p_rows`: -1 marks an empty slot, whose block in p_blocks is not part of P; the block rows named in one block column of one grid row are distinct; one device's 8 block columns of one grid row hold at most 16 stored blocks, and exactly that many on some device; of one device's stored blocks, at most 6 lie in any one aligned range of 8 block rows (rows m * 8 to m * 8 + 7 of the grid row), and exactly that many on some device. `c_rows`: the 3 block rows named in one block column of one grid row are distinct.
All inputs are finite; a program needn't handle non-finite values.
Results may differ from a plain program's by a relative error of at most 0.0003.
Values may be sent and summed in bfloat16 or wider, within the bound.
A program may use at most 64 MiB of HBM per device.

v0:
```python
import jax
import jax.numpy as jnp
from jax import lax
from jax.sharding import PartitionSpec as P

SECTIONS = 4


def spread(block, axis, source):
    block = jnp.where(lax.axis_index(axis) == source, block, jnp.zeros_like(block))
    return lax.psum(block, axis)


def section_terms(a_blocks, a_rows, b_blocks, b_rows, targets, offset):
    col_count = a_rows.shape[1]
    in_panel = b_rows - offset
    b_live = (b_rows >= 0) & (in_panel >= 0) & (in_panel < col_count)
    in_panel = jnp.clip(in_panel, 0, col_count - 1).astype(jnp.int32)
    picked_rows = a_rows[:, in_panel]
    picked = a_blocks[:, in_panel]
    matches = (picked_rows[:, None] == targets[None, :, None, :]) & b_live[None, None]
    selected = jnp.zeros(matches.shape[1:] + picked.shape[3:], jnp.bfloat16)
    for slot_num in range(a_rows.shape[0]):
        selected = selected + jnp.where(
            matches[slot_num][..., None, None], picked[slot_num][None], jnp.zeros((), jnp.bfloat16)
        )
    return jnp.einsum("rejxy,ejyz->rjxz", selected, b_blocks, preferred_element_type=jnp.float32)


def local(p_blocks, p_rows, c_rows):
    blocks = p_blocks[0]
    row_ids = p_rows[0]
    targets = c_rows[0]
    col_count = row_ids.shape[1]
    across = lax.axis_size("col")
    row_count = lax.axis_size("row")
    per_row = col_count * across // row_count
    running = jnp.zeros(
        (targets.shape[0], col_count, blocks.shape[2], blocks.shape[3]), jnp.float32
    )
    for section_num in range(SECTIONS):
        panel_col = section_num * (across // SECTIONS)
        root_row = panel_col * col_count // per_row
        offset = panel_col * col_count % per_row
        a_blocks, a_rows = (spread(blocks, "col", panel_col), spread(row_ids, "col", panel_col))
        b_blocks, b_rows = (spread(blocks, "row", root_row), spread(row_ids, "row", root_row))
        running = running + section_terms(a_blocks, a_rows, b_blocks, b_rows, targets, offset)
    return running[None]


def solution(mesh):
    placed = (P("row", None, "col", None, None), P("row", None, "col"), P("row", None, "col"))
    return jax.shard_map(
        local,
        mesh=mesh,
        in_specs=placed,
        out_specs=P("row", None, "col", None, None),
        check_vma=False,
    )
```

profile of v0, /device:TPU:1, one launch (start us, length us, event | category | flops | bytes accessed | tf_op | source)
XLA Modules:
  0.0 404.4 jit_solution(17562610111916436409)
XLA Ops:
  6.5 1.5 copy.4
  8.0 2.8 select_bitcast_fusion.7
  11.7 10.2 %all-reduce.1 = (s32[3,8]{1,0:T(4,128)S(1)}, s32[3,8]{1,0:T(4,128)S(1)}, s32[3,8]{1,0:T(4,128)S(1)}, s32[3,8]{1,0:T(4,128)S(1)}) all-reduce(s32[3,8]{1,0:T(4,128)S(1)} %get-tuple-element.65, s32[3,8]{1,0:T(4,128)S(1)} %get-tuple-element.66, s32[3,8]{1,0:T(4,128)S(1)} %get-tuple-element.67, ...), channel_id=1, replica_groups=mesh['row'=8,'col'=32] {'row'}, use_global_device_ids=true, to_apply=%region_14.15 | all-reduce | flops 96 | bytes 768 | tf_op jit(solution)/shard_map/psum | solution.py:11
  22.4 131.1 %all-reduce = (s32[3,8]{0,1:T(8,128)S(1)}, s32[3,8]{0,1:T(8,128)S(1)}, s32[3,8]{0,1:T(8,128)S(1)}, s32[3,8]{0,1:T(8,128)S(1)}) all-reduce(s32[3,8]{0,1:T(8,128)S(1)} %bitcast.156, s32[3,8]{0,1:T(8,128)S(1)} %bitcast.155, s32[3,8]{0,1:T(8,128)S(1)} %bitcast.153, s32[3,8]{0,1:T(8,128)S(1)} %bitcast.154), channel_id=1, replica_groups=mesh['row'=8,'col'=32] {'col'}, use_global_device_ids=true, to_apply=%region_13.14 | all-reduce | flops 96 | bytes 768 | tf_op jit(solution)/shard_map/psum | solution.py:11
  157.9 132.7 %all-reduce.7.cloned.1.call-done = (bf16[3,8,128,128]{2,3,0,1:T(8,128)(2,1)}, bf16[3,8,128,128]{2,3,0,1:T(8,128)(2,1)}, bf16[3,8,128,128]{2,3,0,1:T(8,128)(2,1)}, bf16[3,8,128,128]{2,3,0,1:T(8,128)(2,1)}) async-done(((bf16[3,8,128,128]{2,3,0,1:T(8,128)(2,1)}, bf16[3,8,128,128]{2,3,0,1:T(8,128)(2,1)}, bf16[3,8,128,128]{2,3,0,1:T(8,128)(2,1)}, bf16[3,8,128,128]{2,3,0,1:T(8,128)(2,1)}), ...) | async-done | bytes 3145744 | tf_op jit(solution)/shard_map/psum | solution.py:11
  290.6 2.1 gather_fusion.3
  292.7 1.4 slice_bitcast_fusion.8
  294.2 2.4 copy.19
  297.8 1.2 copy.23
  300.0 1.5 slice_bitcast_fusion.5
  301.5 2.4 copy.29
  303.9 2.3 copy.31
  308.4 1.5 slice_bitcast_fusion.2
  309.9 2.4 copy.39
  312.3 2.3 copy.41
  316.9 1.4 slice_bitcast_fusion.11
  318.2 2.5 copy.11
  320.7 2.3 copy.13
  324.2 62.9 %all-reduce.9.cloned.1.call-done = (bf16[3,8,128,128]{2,3,0,1:T(8,128)(2,1)}, bf16[3,8,128,128]{2,3,0,1:T(8,128)(2,1)}, bf16[3,8,128,128]{2,3,0,1:T(8,128)(2,1)}, bf16[3,8,128,128]{2,3,0,1:T(8,128)(2,1)}) async-done(((bf16[3,8,128,128]{2,3,0,1:T(8,128)(2,1)}, bf16[3,8,128,128]{2,3,0,1:T(8,128)(2,1)}, bf16[3,8,128,128]{2,3,0,1:T(8,128)(2,1)}, bf16[3,8,128,128]{2,3,0,1:T(8,128)(2,1)}), ...) | async-done | bytes 3145744 | tf_op jit(solution)/shard_map/psum | solution.py:11
  387.1 2.7 fusion.12
  389.9 1.9 fusion.6
  391.9 1.9 fusion
  393.9 2.0 fusion.36
  396.0 1.6 copy.44
  (106 shorter events, 13.5 us)
Async XLA Ops:
  6.5 284.1 %all-reduce.7.cloned.1.call-start = ((), (), s32[]{:S(2)}) async-start(), calls=%async_computation | async-start | bytes 6291456 | tf_op jit(solution)/shard_map/psum | solution.py:11
  10.9 145.5 %copy-start.19 = (s32[1,3,8]{2,0,1:T(1,128)S(1)}, s32[1,3,8]{2,0,1:T(1,128)}, u32[]{:S(2)}) copy-start(s32[1,3,8]{2,0,1:T(1,128)} %param.5) | copy-start | bytes 292
  10.9 376.2 %all-reduce.9.cloned.1.call-start = ((), (), s32[]{:S(2)}) async-start(), calls=%async_computation.1 | async-start | bytes 6291456 | tf_op jit(solution)/shard_map/psum | solution.py:11
  294.2 3.6 copy-start.3
  294.2 4.8 %copy-start.2 = (bf16[3,8,128,128]{2,3,0,1:T(8,128)(2,1)S(1)}, bf16[3,8,128,128]{2,3,0,1:T(8,128)(2,1)}, u32[]{:S(2)}) copy-start(bf16[3,8,128,128]{2,3,0,1:T(8,128)(2,1)} %get-tuple-element.14) | copy-start | bytes 2359300
  301.5 4.7 %copy-start.4 = (bf16[3,8,128,128]{2,3,1,0:T(8,128)(2,1)S(1)}, bf16[3,8,128,128]{2,3,1,0:T(8,128)(2,1)}, u32[]{:S(2)}) copy-start(bf16[3,8,128,128]{2,3,1,0:T(8,128)(2,1)} %get-tuple-element.29) | copy-start | bytes 2359300
  301.5 5.9 %copy-start.1 = (bf16[3,8,128,128]{2,3,0,1:T(8,128)(2,1)S(1)}, bf16[3,8,128,128]{2,3,0,1:T(8,128)(2,1)}, u32[]{:S(2)}) copy-start(bf16[3,8,128,128]{2,3,0,1:T(8,128)(2,1)} %get-tuple-element.13) | copy-start | bytes 2359300
  309.9 4.7 %copy-start.5 = (bf16[3,8,128,128]{2,3,1,0:T(8,128)(2,1)S(1)}, bf16[3,8,128,128]{2,3,1,0:T(8,128)(2,1)}, u32[]{:S(2)}) copy-start(bf16[3,8,128,128]{2,3,1,0:T(8,128)(2,1)} %get-tuple-element.32) | copy-start | bytes 2359300
  309.9 5.9 %copy-start = (bf16[3,8,128,128]{2,3,0,1:T(8,128)(2,1)S(1)}, bf16[3,8,128,128]{2,3,0,1:T(8,128)(2,1)}, u32[]{:S(2)}) copy-start(bf16[3,8,128,128]{2,3,0,1:T(8,128)(2,1)} %get-tuple-element.16) | copy-start | bytes 2359300
  318.2 68.8 %copy-start.6 = (bf16[3,8,128,128]{3,2,0,1:T(8,128)(2,1)S(1)}, bf16[3,8,128,128]{3,2,0,1:T(8,128)(2,1)}, u32[]{:S(2)}) copy-start(bf16[3,8,128,128]{3,2,0,1:T(8,128)(2,1)} %copy.19) | copy-start | bytes 2359300
  318.2 68.8 %copy-start.7 = (bf16[3,8,128,128]{3,2,0,1:T(8,128)(2,1)S(1)}, bf16[3,8,128,128]{3,2,0,1:T(8,128)(2,1)}, u32[]{:S(2)}) copy-start(bf16[3,8,128,128]{3,2,0,1:T(8,128)(2,1)} %copy.21) | copy-start | bytes 2359300
  318.2 68.8 %copy-start.8 = (bf16[3,8,128,128]{3,2,0,1:T(8,128)(2,1)S(1)}, bf16[3,8,128,128]{3,2,0,1:T(8,128)(2,1)}, u32[]{:S(2)}) copy-start(bf16[3,8,128,128]{3,2,0,1:T(8,128)(2,1)} %copy.23) | copy-start | bytes 2359300
  387.1 2.8 copy-start.9
  387.1 2.8 copy-start.10
  387.1 2.8 copy-start.11
  387.1 2.8 copy-start.22
  389.9 2.0 copy-start.12
  389.9 2.0 copy-start.13
  389.9 2.0 copy-start.14
  389.9 2.0 copy-start.21
  391.9 2.0 copy-start.15
  391.9 2.0 copy-start.16
  391.9 2.0 copy-start.17
  391.9 2.0 copy-start.20
  (1 other events, 0.8 us)
Sparse Core Ops, SparseCore 0:
  11.0 279.5 all-reduce.6
  293.8 93.2 all-reduce.8
where the time goes:
time: 405 us; the launch traced here: 404 us
  waiting for transfers between devices  196 us (48%)
  blocking collectives  141 us (35%)
  local copies, waits for them, and re-layouts  41.5 us (10%)
  between operations  13.8 us (3%)
  matrix products  8.62 us (2%)
    psum x2, waiting for transfers between devices, spread(): return lax.psum(block, axis)  196 us
    psum x2, blocking collectives, spread(): return lax.psum(block, axis)  141 us
    broadcast_in_dim x32, local copies, waits for them, and re-layouts, section_terms(): jnp.where(matches[slot_num][..., None, None], picked[slot_num][None], jnp...  29.8 us
    dot_general x4, matrix products, section_terms(): jnp.einsum('rejxy,ejyz->rjxz', selected, b_blocks, preferred_element_type...  8.62 us
  transfers between devices with their start and end apart: 2, of which 2 were waited for; matrix products, arithmetic and copies ran while one was open for 9% of the time, Pallas kernels for 0%

commit v1 on v0

v1 whole, which is shorter than its diff:
```python
import functools

import jax
import jax.numpy as jnp
from jax import lax
from jax.experimental import pallas as pl
from jax.experimental.pallas import tpu as pltpu
from jax.sharding import PartitionSpec as P

MESH = pl.DeviceIdType.MESH
BLK = 128
NCOL = 8
SLOTS = 3
NA = 16
NB = 6
HALF = NA // 2
AC = 4
AB = HALF // AC
BC = 2
BB = NB // BC
RX, RZ = 4, 8


def kernel(p_hbm, rows_s, targets_s, rows_v, out_ref, *scratch):
    a_bufs = scratch[0:4]
    tab_s = scratch[4:8]
    (b_buf, tab_v, bm_v, bm_s, p_v, ids, a_pick, b_pick, p_sem,
     a_recv, a_srecv, a_ssend, a_send, t_recv, t_send, t_sib,
     b_recv, b_send, m_recv, m_send, loc_sem, bm_sem) = scratch[8:]

    r, c = lax.axis_index("row"), lax.axis_index("col")
    x, y_lo = r % RX, r // RX
    core, z, y_hi = c % 2, (c // 2) % RZ, c // (2 * RZ)

    def device(x, y_lo, y_hi, z, core):
        return (y_lo * RX + x, (y_hi * RZ + z) * 2 + core)

    z_up = device(x, y_lo, y_hi, (z + 1) % RZ, core)
    z_down = device(x, y_lo, y_hi, (z + RZ - 1) % RZ, core)
    y_far = device(x, y_lo, 1 - y_hi, z, core)
    sib = device(x, y_lo, y_hi, z, 1 - core)
    x_up = device((x + 1) % RX, y_lo, y_hi, z, core)
    x_down = device((x + RX - 1) % RX, y_lo, y_hi, z, core)
    y_near = device(x, 1 - y_lo, y_hi, z, core)
    partners = (z_up, z_down, y_far, sib, x_up, x_down, y_near)

    barrier = pltpu.get_barrier_semaphore()
    for partner in partners:
        pl.semaphore_signal(barrier, inc=1, device_id=partner, device_id_type=MESH)

    a_root = (z % (RZ // 2) == 0) & (core == 0)
    b_root = x % (RX // 2) == 0
    fetch = pltpu.make_async_copy(p_hbm, p_v, p_sem)

    @pl.when(a_root | b_root)
    def _():
        fetch.start()
        ids[...] = jnp.full((8, 128), -1, jnp.int32)
        ids[0:SLOTS, 0:NCOL] = rows_v[...]

    for u in range(4):
        a_bufs[u][NA] = jnp.zeros((BLK, BLK), jnp.bfloat16)

    lane = lax.broadcasted_iota(jnp.int32, (8, 128), 1)
    sub = lax.broadcasted_iota(jnp.int32, (8, 128), 0)

    def running(stored):
        counts, total = [], jnp.int32(0)
        for e in range(SLOTS):
            for j in range(NCOL):
                total = total + stored(rows_s[e, j])
                counts.append(total)
        return counts

    def pick(counts, slots, out):
        for i in range(slots):
            place = jnp.int32(0)
            for count in counts[:-1]:
                place = place + jnp.where(count <= i, 1, 0)
            out[i] = place

    def prefix(ones):
        total = ones + pltpu.roll(ones, 1, 1)
        total = total + pltpu.roll(total, 2, 1)
        return total + pltpu.roll(total, 4, 1)

    @pl.when(b_root)
    def _():
        counts = running(lambda row: jnp.where((row >= 0) & (row < NCOL), 1, 0))
        pick(counts, NB, b_pick)
        held = ids[...]
        live = (held >= 0) & (held < NCOL)
        ones = jnp.where(live, 1, 0)
        base = jnp.where(sub == 1, counts[NCOL - 1], jnp.where(sub == 2, counts[2 * NCOL - 1], 0))
        v = x // (RX // 2)
        bm_v[v, 0] = jnp.where(live, held, NCOL)
        bm_v[v, 1] = jnp.where(live, jnp.minimum(prefix(ones) - ones + base, NB - 1), 0)

    @pl.when(a_root)
    def _():
        counts = running(lambda row: jnp.where(row >= 0, 1, 0))
        pick(counts, NA, a_pick)
        table = jnp.full((8, 128), NA, jnp.int32)
        wanted = (lane // 32) * 8 + sub
        for e in range(SLOTS):
            one = jnp.broadcast_to(ids[e:e + 1, :], (8, 128))
            two = jnp.maximum(one, pltpu.roll(one, 32, 1))
            four = jnp.maximum(two, pltpu.roll(two, 64, 1))
            ones = jnp.where(four >= 0, 1, 0)
            base = counts[e * NCOL - 1] if e else 0
            table = jnp.where(four == wanted, jnp.minimum(prefix(ones) - ones + base, NA), table)
        tab_v[z // (RZ // 2)] = table

    @pl.when(a_root | b_root)
    def _():
        fetch.wait()

    @pl.when(b_root)
    def _():
        for i in range(NB):
            b_buf[x // (RX // 2), i] = p_v[b_pick[i]]

    for v in range(2):
        @pl.when(a_root & (z == v * (RZ // 2)))
        def _(v=v):
            for i in range(NA):
                a_bufs[v][i] = p_v[a_pick[i]]

    pl.semaphore_wait(barrier, len(partners))

    def remote(src, dst, send, recv, to):
        return pltpu.make_async_remote_copy(
            src_ref=src, dst_ref=dst, send_sem=send, recv_sem=recv, device_id=to, device_id_type=MESH
        )

    def a_steps(u, k):
        flag, v = divmod(u, 2)
        d = (z + RZ - v * (RZ // 2)) % RZ
        first = k < AC // 2
        mine = pl.ds(core * HALF + k * AB, AB)
        other = pl.ds((1 - core) * HALF + k * AB, AB)
        part, far = a_bufs[u].at[mine], a_bufs[u].at[other]
        up = (d <= 3) if first else (d <= 2)
        down = (d == 0) | (d >= (6 if first else 5))
        out = []
        if flag == 0:
            root = (d == 0) & (core == 0)
            out.append((root, remote(far, far, a_ssend.at[u, AC + k], a_recv.at[u, k], sib)))
        out.append((up, remote(part, part, a_send.at[0, u, k], a_recv.at[u, k], z_up)))
        out.append((down, remote(part, part, a_send.at[1, u, k], a_recv.at[u, k], z_down)))
        if flag == 0:
            across = a_bufs[u + 2].at[mine]
            out.append((d == 0, remote(part, across, a_send.at[2, u, k], a_recv.at[u + 2, k], y_far)))
            beside = (d != 0) | (core == 0)
        else:
            beside = None
        out.append((beside, remote(part, part, a_ssend.at[u, k], a_srecv.at[u, k], sib)))
        return out

    def t_steps(u):
        flag, v = divmod(u, 2)
        d = (z + RZ - v * (RZ // 2)) % RZ
        part = tab_v.at[u]
        out = []
        if flag == 0:
            root = (d == 0) & (core == 0)
            out.append((root, remote(part, part, t_sib.at[u], t_recv.at[u], sib)))
        out.append((d <= 3, remote(part, part, t_send.at[0, u], t_recv.at[u], z_up)))
        out.append(((d == 0) | (d >= 6), remote(part, part, t_send.at[1, u], t_recv.at[u], z_down)))
        if flag == 0:
            out.append((d == 0, remote(part, tab_v.at[u + 2], t_send.at[2, u], t_recv.at[u + 2], y_far)))
        return out

    def b_steps(w, k):
        flag, v = divmod(w, 2)
        d = (x + RX - v * (RX // 2)) % RX
        if k is None:
            part, across = bm_v.at[w], bm_v.at[w % 2 + 2]
            send = lambda n: m_send.at[n, w]
            recv = lambda w: m_recv.at[w]
            up, down = d <= 1, d == 0
        else:
            part, across = b_buf.at[w, pl.ds(k * BB, BB)], b_buf.at[w % 2 + 2, pl.ds(k * BB, BB)]
            send = lambda n: b_send.at[n, w, k]
            recv = lambda w: b_recv.at[w, k]
            up = (d <= 1) if k < BC // 2 else (d == 0)
            down = (d == 0) if k < BC // 2 else ((d == 0) | (d == 3))
        out = [(up, remote(part, part, send(0), recv(w), x_up)), (down, remote(part, part, send(1), recv(w), x_down))]
        if flag == 0:
            out.append((d == 0, remote(part, across, send(2), recv(w + 2), y_near)))
        return out

    def start(steps):
        for condition, copy in steps:
            if condition is None:
                copy.start()
            else:
                pl.when(condition)(copy.start)

    def finish(steps):
        for condition, copy in steps:
            if condition is None:
                copy.wait_send()
            else:
                pl.when(condition)(copy.wait_send)

    def arrived(buf, sem):
        remote(buf, buf, loc_sem.at[0], sem, sib).wait_recv()

    def relay_a(u, k):
        flag, v = divmod(u, 2)
        mine = a_bufs[u].at[pl.ds(core * HALF + k * AB, AB)]
        if flag == 0:
            @pl.when((z != v * (RZ // 2)) | (core != 0))
            def _():
                arrived(mine, a_recv.at[u, k])
        else:
            arrived(mine, a_recv.at[u, k])
        start(a_steps(u, k))

    def relay_t(u):
        flag, v = divmod(u, 2)
        if flag == 0:
            @pl.when((z != v * (RZ // 2)) | (core != 0))
            def _():
                arrived(tab_v.at[u], t_recv.at[u])
        else:
            arrived(tab_v.at[u], t_recv.at[u])
        start(t_steps(u))
        pltpu.make_async_copy(tab_v.at[u], tab_s[u], loc_sem.at[u]).start()

    def relay_all(u):
        relay_t(u)
        for k in range(AC):
            relay_a(u, k)

    def b_wait(w):
        arrived(bm_v.at[w], m_recv.at[w])
        for k in range(BC):
            arrived(b_buf.at[w, pl.ds(k * BB, BB)], b_recv.at[w, k])

    def b_distance(w):
        return (x + RX - (w % 2) * (RX // 2)) % RX

    def relay_b(w, kind):
        d = b_distance(w)

        @pl.when((d == 0) if kind == "root" else (d % 2 == 1))
        def _():
            if kind == "root" and w < 2:
                start(b_steps(w, None))
                for k in range(BC):
                    start(b_steps(w, k))
            else:
                arrived(bm_v.at[w], m_recv.at[w])
                start(b_steps(w, None))
                for k in range(BC):
                    arrived(b_buf.at[w, pl.ds(k * BB, BB)], b_recv.at[w, k])
                    start(b_steps(w, k))

    for w in (0, 1):
        relay_b(w, "root")

    def b_first():
        for w in (2, 3):
            relay_b(w, "root")
        for w in (0, 1):
            relay_b(w, "odd")

    def b_second():
        for w in (2, 3):
            relay_b(w, "odd")

    for near in (0, 1):
        @pl.when((z % 4 != 2) & ((z + 2) // 4 % 2 == near))
        def _(near=near):
            relay_all(near)
            b_first()
            relay_all(near + 2)
            relay_all(1 - near)
            b_second()
            relay_all(3 - near)

    @pl.when(z % 4 == 2)
    def _():
        for pair in (0, 2):
            relay_t(pair)
            relay_t(pair + 1)
            for k in range(AC):
                relay_a(pair, k)
                relay_a(pair + 1, k)
            (b_second if pair else b_first)()

    for w in range(4):
        pl.when(b_distance(w) == 2)(functools.partial(b_wait, w))
    to_smem = pltpu.make_async_copy(bm_v, bm_s, bm_sem)
    to_smem.start()
    to_smem.wait()

    for u in range(4):
        flag, v = divmod(u, 2)
        pltpu.make_async_copy(tab_v.at[u], tab_s[u], loc_sem.at[u]).wait()
        other = lambda k: a_bufs[u].at[pl.ds((1 - core) * HALF + k * AB, AB)]
        for k in range(AC):
            if flag == 0:
                @pl.when((z != v * (RZ // 2)) | (core != 0))
                def _():
                    arrived(other(k), a_srecv.at[u, k])
            else:
                arrived(other(k), a_srecv.at[u, k])
        w = (flag + y_hi + y_lo) % 2 * 2 + v
        panel, table = a_bufs[u], tab_s[u]

        def column(j, _):
            places = []
            for s in range(SLOTS):
                target = targets_s[s, j]
                places.append((target % 8, target // 8 * 32))
            left, right = [], []
            for e in range(SLOTS):
                at = bm_s[w, 0, e, j]
                right.append(b_buf[w, bm_s[w, 1, e, j]])
                left.append(jnp.concatenate([panel[table[low, high + at]] for low, high in places], axis=0))
            term = jnp.dot(
                jnp.concatenate(left, axis=1), jnp.concatenate(right, axis=0), preferred_element_type=jnp.float32
            )
            for s in range(SLOTS):
                piece = term[s * BLK:(s + 1) * BLK]
                out_ref[s, j] = piece if u == 0 else out_ref[s, j] + piece
            return 0

        lax.fori_loop(0, NCOL, column, 0)

    for u in range(4):
        finish(t_steps(u))
        for k in range(AC):
            finish(a_steps(u, k))
    for w in range(4):
        finish(b_steps(w, None))
        for k in range(BC):
            finish(b_steps(w, k))


def local(p_blocks, p_rows, c_rows):
    blocks = p_blocks.reshape(SLOTS * NCOL, BLK, BLK)
    rows, targets = p_rows[0], c_rows[0]
    dma = pltpu.SemaphoreType.DMA
    out = pl.pallas_call(
        kernel,
        out_shape=jax.ShapeDtypeStruct((SLOTS, NCOL, BLK, BLK), jnp.float32),
        in_specs=[
            pl.BlockSpec(memory_space=pl.ANY),
            pl.BlockSpec(memory_space=pltpu.SMEM),
            pl.BlockSpec(memory_space=pltpu.SMEM),
            pl.BlockSpec(memory_space=pltpu.VMEM),
        ],
        out_specs=pl.BlockSpec(memory_space=pltpu.VMEM),
        scratch_shapes=[pltpu.VMEM((NA + 1, BLK, BLK), jnp.bfloat16)] * 4
        + [pltpu.SMEM((8, 128), jnp.int32)] * 4
        + [
            pltpu.VMEM((4, NB, BLK, BLK), jnp.bfloat16),
            pltpu.VMEM((4, 8, 128), jnp.int32),
            pltpu.VMEM((4, 2, 8, 128), jnp.int32),
            pltpu.SMEM((4, 2, 8, 128), jnp.int32),
            pltpu.VMEM((SLOTS * NCOL, BLK, BLK), jnp.bfloat16),
            pltpu.VMEM((8, 128), jnp.int32),
            pltpu.SMEM((NA,), jnp.int32),
            pltpu.SMEM((NB,), jnp.int32),
            dma,
            dma((4, AC)), dma((4, AC)), dma((4, 2 * AC)), dma((3, 4, AC)),
            dma((4,)), dma((3, 4)), dma((4,)),
            dma((4, BC)), dma((3, 4, BC)), dma((4,)), dma((3, 4)),
            dma((4,)), dma,
        ],
        compiler_params=pltpu.CompilerParams(
            collective_id=0, has_side_effects=True, vmem_limit_bytes=32 * 1024 * 1024
        ),
        name="panels",
    )(blocks, rows, targets, rows)
    return out[None]


def solution(mesh):
    placed = (P("row", None, "col", None, None), P("row", None, "col"), P("row", None, "col"))
    return jax.shard_map(
        local,
        mesh=mesh,
        in_specs=placed,
        out_specs=P("row", None, "col", None, None),
        check_vma=False,
    )
```

time: 405 us -> 48.4 us (0.12)
  the two profiles are of different devices: /device:TPU:1 before, /device:TPU:8 now
where the time goes in v1:
time: 48.4 us; the launch traced here: 48.3 us
  Pallas kernels  45.3 us (94%)
  local copies, waits for them, and re-layouts  2.98 us (6%)
    pallas_call x1, Pallas kernels, local(): pl.pallas_call(kernel, out_shape=jax.ShapeDtypeStruct((SLOTS, NCOL, BLK,...  45.3 us
    unnamed x4, local copies, waits for them, and re-layouts  2.98 us

profile of v1, /device:TPU:8, one launch (start us, length us, event | category | flops | bytes accessed | tf_op | source)
XLA Modules:
  0.0 48.3 jit_solution(1230892097439660372)
XLA Ops:
  0.0 0.7 %copy_bitcast_fusion = (s32[3,8]{1,0:T(4,128)S(1)}, s32[3,8]{1,0:T(4,128)S(1)}) fusion(s32[1,3,8]{2,0,1:T(1,128)} %param.5, s32[1,3,8]{2,0,1:T(1,128)} %param.4), kind=kLoop, calls=%fused_computation | loop fusion | bytes 384
  0.7 0.0 copy-start
  0.7 1.1 %copy-done = bf16[1,3,8,128,128]{4,3,2,1,0:T(8,128)(2,1)S(1)} copy-done((bf16[1,3,8,128,128]{4,3,2,1,0:T(8,128)(2,1)S(1)}, bf16[1,3,8,128,128]{4,3,2,1,0:T(8,128)(2,1)}, u32[]{:S(2)}) %copy-start) | copy-done | bytes 786456
  1.8 45.3 %panels.1 = f32[3,8,128,128]{3,2,1,0:T(8,128)S(1)} custom-call(bf16[24,128,128]{2,1,0:T(8,128)(2,1)S(1)} %bitcast.7, s32[3,8]{1,0:T(4,128)S(1)} %get-tuple-element.6.rows_s.rows_v, s32[3,8]{1,0:T(4,128)S(1)} %get-tuple-element.5.targets_s, s32[3,8]{1,0:T(4,128)S(1)} %get-tuple-element.6.rows_s.rows_v), custom_call_target="tpu_custom_call" | custom-call | tf_op jit(solution)/shard_map/panels/pallas_call | solution.py:348
  47.1 1.1 %copy.9 = f32[1,3,8,128,128]{4,3,2,1,0:T(8,128)} copy(f32[1,3,8,128,128]{4,3,2,1,0:T(8,128)S(1)} %bitcast.6) | data formatting | bytes 3145728
Async XLA Ops:
  0.7 1.1 %copy-start = (bf16[1,3,8,128,128]{4,3,2,1,0:T(8,128)(2,1)S(1)}, bf16[1,3,8,128,128]{4,3,2,1,0:T(8,128)(2,1)}, u32[]{:S(2)}) copy-start(bf16[1,3,8,128,128]{4,3,2,1,0:T(8,128)(2,1)} %param.3) | copy-start | bytes 2359300

commit v2 on v1

--- a/solution.py
+++ b/solution.py
@@ -14,19 +14,20 @@
 NA = 16
 NB = 6
 HALF = NA // 2
-AC = 4
+AC = 8
 AB = HALF // AC
+EARLY = AC // 2
 BC = 2
 BB = NB // BC
 RX, RZ = 4, 8
 
 
-def kernel(p_hbm, rows_s, targets_s, rows_v, out_ref, *scratch):
+def kernel(p_hbm, rows_hbm, targets_hbm, out_hbm, *scratch):
     a_bufs = scratch[0:4]
     tab_s = scratch[4:8]
     (b_buf, tab_v, bm_v, bm_s, p_v, ids, a_pick, b_pick, p_sem,
      a_recv, a_srecv, a_ssend, a_send, t_recv, t_send, t_sib,
-     b_recv, b_send, m_recv, m_send, loc_sem, bm_sem) = scratch[8:]
+     b_recv, b_send, m_recv, m_send, loc_sem, bm_sem, rows_s, targets_s, rows_v, in_sem, acc, out_sem) = scratch[8:]
 
     r, c = lax.axis_index("row"), lax.axis_index("col")
     x, y_lo = r % RX, r // RX
@@ -44,19 +45,32 @@
     y_near = device(x, 1 - y_lo, y_hi, z, core)
     partners = (z_up, z_down, y_far, sib, x_up, x_down, y_near)
 
+    row_copy = pltpu.make_async_copy(rows_hbm, rows_s, in_sem.at[0])
+    row_copy_v = pltpu.make_async_copy(rows_hbm, rows_v, in_sem.at[1])
+    target_copy = pltpu.make_async_copy(targets_hbm, targets_s, in_sem.at[2])
+    a_root = (z % (RZ // 2) == 0) & (core == 0)
+    b_root = x % (RX // 2) == 0
+    fetch = pltpu.make_async_copy(p_hbm, p_v, p_sem)
+
+    @pl.when(a_root | b_root)
+    def _():
+        row_copy.start()
+        row_copy_v.start()
+        fetch.start()
+
+    target_copy.start()
+
     barrier = pltpu.get_barrier_semaphore()
     for partner in partners:
         pl.semaphore_signal(barrier, inc=1, device_id=partner, device_id_type=MESH)
 
-    a_root = (z % (RZ // 2) == 0) & (core == 0)
-    b_root = x % (RX // 2) == 0
-    fetch = pltpu.make_async_copy(p_hbm, p_v, p_sem)
-
     @pl.when(a_root | b_root)
     def _():
-        fetch.start()
+        row_copy.wait()
+        row_copy_v.wait()
         ids[...] = jnp.full((8, 128), -1, jnp.int32)
-        ids[0:SLOTS, 0:NCOL] = rows_v[...]
+        for e in range(SLOTS):
+            ids[e:e + 1, 0:NCOL] = rows_v[e]
 
     for u in range(4):
         a_bufs[u][NA] = jnp.zeros((BLK, BLK), jnp.bfloat16)
@@ -68,7 +82,7 @@
         counts, total = [], jnp.int32(0)
         for e in range(SLOTS):
             for j in range(NCOL):
-                total = total + stored(rows_s[e, j])
+                total = total + stored(rows_s[e, 0, j])
                 counts.append(total)
         return counts
 
@@ -136,25 +150,28 @@
     def a_steps(u, k):
         flag, v = divmod(u, 2)
         d = (z + RZ - v * (RZ // 2)) % RZ
-        first = k < AC // 2
         mine = pl.ds(core * HALF + k * AB, AB)
         other = pl.ds((1 - core) * HALF + k * AB, AB)
         part, far = a_bufs[u].at[mine], a_bufs[u].at[other]
-        up = (d <= 3) if first else (d <= 2)
-        down = (d == 0) | (d >= (6 if first else 5))
-        out = []
-        if flag == 0:
-            root = (d == 0) & (core == 0)
-            out.append((root, remote(far, far, a_ssend.at[u, AC + k], a_recv.at[u, k], sib)))
-        out.append((up, remote(part, part, a_send.at[0, u, k], a_recv.at[u, k], z_up)))
-        out.append((down, remote(part, part, a_send.at[1, u, k], a_recv.at[u, k], z_down)))
+        even = k % 2 == 0
+        up = (d <= 2) | ((d == 3) & even)
+        down = (d == 0) | (d >= 6) | ((d == 5) & (k % 2 == 1))
+        if flag:
+            up, down = up & (k >= EARLY), down & (k >= EARLY)
+        out = dict(
+            up=(up, remote(part, part, a_send.at[0, u, k], a_recv.at[u, k], z_up)),
+            down=(down, remote(part, part, a_send.at[1, u, k], a_recv.at[u, k], z_down)),
+            side=(None, remote(part, part, a_ssend.at[u, k], a_srecv.at[u, k], sib)),
+        )
         if flag == 0:
             across = a_bufs[u + 2].at[mine]
-            out.append((d == 0, remote(part, across, a_send.at[2, u, k], a_recv.at[u + 2, k], y_far)))
-            beside = (d != 0) | (core == 0)
-        else:
-            beside = None
-        out.append((beside, remote(part, part, a_ssend.at[u, k], a_srecv.at[u, k], sib)))
+            out["side"] = ((d != 0) | (core == 0), out["side"][1])
+            out["across"] = (
+                (d == 0) | (k < EARLY), remote(part, across, a_send.at[2, u, k], a_recv.at[u + 2, k], y_far)
+            )
+            out["far"] = (
+                (d == 0) & (core == 0), remote(far, far, a_ssend.at[u, AC + k], a_recv.at[u, k], sib)
+            )
         return out
 
     def t_steps(u):
@@ -207,16 +224,65 @@
     def arrived(buf, sem):
         remote(buf, buf, loc_sem.at[0], sem, sib).wait_recv()
 
+    def loop(body, low=0, high=AC):
+        def step(k, _):
+            body(k)
+            return 0
+
+        lax.fori_loop(low, high, step, 0)
+
+    def mine(u, k):
+        return a_bufs[u].at[pl.ds(core * HALF + k * AB, AB)]
+
     def relay_a(u, k):
-        flag, v = divmod(u, 2)
-        mine = a_bufs[u].at[pl.ds(core * HALF + k * AB, AB)]
-        if flag == 0:
-            @pl.when((z != v * (RZ // 2)) | (core != 0))
+        arrived(mine(u, k), a_recv.at[u, k])
+        steps = a_steps(u, k)
+        steps.pop("far", None)
+        start(steps.values())
+
+    def relay_own(u, between=None):
+        root = z == u * (RZ // 2)
+
+        @pl.when(z != u * (RZ // 2))
+        def _():
+            if between is None:
+                loop(lambda k: relay_a(u, k))
+            else:
+                loop(lambda k: relay_a(u, k), 0, 3)
+                between()
+                loop(lambda k: relay_a(u, k), 3)
+
+        @pl.when(root)
+        def _():
+            @pl.when(core == 0)
             def _():
-                arrived(mine, a_recv.at[u, k])
-        else:
-            arrived(mine, a_recv.at[u, k])
-        start(a_steps(u, k))
+                loop(lambda k: a_steps(u, k)["far"][1].start())
+
+            @pl.when(core == 1)
+            def _():
+                loop(lambda k: arrived(mine(u, k), a_recv.at[u, k]))
+
+            def send(k):
+                steps = a_steps(u, k)
+                steps["up"][1].start()
+                steps["down"][1].start()
+                a_steps(u, (k + EARLY) % AC)["across"][1].start()
+                start([steps["side"]])
+
+            loop(send)
+            if between is not None:
+                between()
+
+    def relay_far(u, also=None, low=0, high=AC):
+        def step(k):
+            relay_a(u, (k + EARLY) % AC)
+            if also is not None:
+                also(k)
+
+        loop(step, low, high)
+
+    def send_out(j):
+        return pltpu.make_async_copy(acc.at[:, j], out_hbm.at[:, j], out_sem.at[j])
 
     def relay_t(u):
         flag, v = divmod(u, 2)
@@ -228,11 +294,6 @@
             arrived(tab_v.at[u], t_recv.at[u])
         start(t_steps(u))
         pltpu.make_async_copy(tab_v.at[u], tab_s[u], loc_sem.at[u]).start()
-
-    def relay_all(u):
-        relay_t(u)
-        for k in range(AC):
-            relay_a(u, k)
 
     def b_wait(w):
         arrived(bm_v.at[w], m_recv.at[w])
@@ -271,90 +332,142 @@
         for w in (2, 3):
             relay_b(w, "odd")
 
+    def b_ready():
+        for w in range(4):
+            pl.when(b_distance(w) == 2)(functools.partial(b_wait, w))
+        to_smem = pltpu.make_async_copy(bm_v, bm_s, bm_sem)
+        to_smem.start()
+        to_smem.wait()
+
+    def a_ready(u):
+        pltpu.make_async_copy(tab_v.at[u], tab_s[u], loc_sem.at[u]).wait()
+
+        def wait(k):
+            arrived(a_bufs[u].at[pl.ds((1 - core) * HALF + k * AB, AB)], a_srecv.at[u, k])
+
+        if u < 2:
+            @pl.when((z != u * (RZ // 2)) | (core != 0))
+            def _():
+                loop(wait)
+        else:
+            loop(wait)
+
+    def column(u, j, first=False):
+        flag, v = divmod(u, 2)
+        w = (flag + y_hi + y_lo) % 2 * 2 + v
+        panel, table = a_bufs[u], tab_s[u]
+        places = []
+        for s in range(SLOTS):
+            target = targets_s[s, 0, j]
+            places.append((target % 8, target // 8 * 32))
+        left, right = [], []
+        for e in range(SLOTS):
+            at = bm_s[w, 0, e, j]
+            right.append(b_buf[w, bm_s[w, 1, e, j]])
+            left.append(jnp.concatenate([panel[table[low, high + at]] for low, high in places], axis=0))
+        term = jnp.dot(
+            jnp.concatenate(left, axis=1), jnp.concatenate(right, axis=0), preferred_element_type=jnp.float32
+        )
+        for s in range(SLOTS):
+            piece = term[s * BLK:(s + 1) * BLK]
+            acc[s, j] = piece if first else acc[s, j] + piece
+
+    target_copy.wait()
     for near in (0, 1):
         @pl.when((z % 4 != 2) & ((z + 2) // 4 % 2 == near))
         def _(near=near):
-            relay_all(near)
-            b_first()
-            relay_all(near + 2)
-            relay_all(1 - near)
+            relay_t(near)
+            relay_own(near, b_first)
+            relay_t(near + 2)
+            relay_far(near + 2, high=EARLY)
             b_second()
-            relay_all(3 - near)
+            relay_far(near + 2, low=EARLY)
+            relay_t(1 - near)
+            relay_own(1 - near)
+            b_ready()
+            relay_t(3 - near)
+            for u in (near, near + 2, 1 - near):
+                a_ready(u)
+
+            def also(k):
+                column(near, k, True)
+                column(near + 2, k)
+                column(1 - near, k)
+
+            relay_far(3 - near, also)
+            a_ready(3 - near)
+
+            def last(j):
+                column(3 - near, j)
+                send_out(j).start()
+
+            loop(last)
 
     @pl.when(z % 4 == 2)
     def _():
-        for pair in (0, 2):
-            relay_t(pair)
-            relay_t(pair + 1)
-            for k in range(AC):
-                relay_a(pair, k)
-                relay_a(pair + 1, k)
-            (b_second if pair else b_first)()
-
-    for w in range(4):
-        pl.when(b_distance(w) == 2)(functools.partial(b_wait, w))
-    to_smem = pltpu.make_async_copy(bm_v, bm_s, bm_sem)
-    to_smem.start()
-    to_smem.wait()
-
-    for u in range(4):
-        flag, v = divmod(u, 2)
-        pltpu.make_async_copy(tab_v.at[u], tab_s[u], loc_sem.at[u]).wait()
-        other = lambda k: a_bufs[u].at[pl.ds((1 - core) * HALF + k * AB, AB)]
-        for k in range(AC):
-            if flag == 0:
-                @pl.when((z != v * (RZ // 2)) | (core != 0))
-                def _():
-                    arrived(other(k), a_srecv.at[u, k])
-            else:
-                arrived(other(k), a_srecv.at[u, k])
-        w = (flag + y_hi + y_lo) % 2 * 2 + v
-        panel, table = a_bufs[u], tab_s[u]
-
-        def column(j, _):
-            places = []
-            for s in range(SLOTS):
-                target = targets_s[s, j]
-                places.append((target % 8, target // 8 * 32))
-            left, right = [], []
-            for e in range(SLOTS):
-                at = bm_s[w, 0, e, j]
-                right.append(b_buf[w, bm_s[w, 1, e, j]])
-                left.append(jnp.concatenate([panel[table[low, high + at]] for low, high in places], axis=0))
-            term = jnp.dot(
-                jnp.concatenate(left, axis=1), jnp.concatenate(right, axis=0), preferred_element_type=jnp.float32
-            )
-            for s in range(SLOTS):
-                piece = term[s * BLK:(s + 1) * BLK]
-                out_ref[s, j] = piece if u == 0 else out_ref[s, j] + piece
-            return 0
-
-        lax.fori_loop(0, NCOL, column, 0)
+        b_first()
+        for u in (0, 1):
+            relay_t(u)
+
+        def own(k):
+            relay_a(0, k)
+            relay_a(1, k)
+
+        loop(own)
+        b_second()
+        for u in (2, 3):
+            relay_t(u)
+
+        def far(k):
+            relay_a(2, (k + EARLY) % AC)
+            relay_a(3, (k + EARLY) % AC)
+
+        loop(far, 0, EARLY)
+        b_ready()
+        a_ready(0)
+        a_ready(1)
+
+        def far_and_columns(k):
+            far(k)
+            for part in range(2):
+                j = (k - EARLY) * 2 + part
+                column(0, j, True)
+                column(1, j)
+
+        loop(far_and_columns, EARLY)
+        a_ready(2)
+        a_ready(3)
+
+        def last(j):
+            column(2, j)
+            column(3, j)
+            send_out(j).start()
+
+        loop(last)
 
     for u in range(4):
         finish(t_steps(u))
-        for k in range(AC):
-            finish(a_steps(u, k))
+        loop(lambda k: finish(a_steps(u, k).values()))
     for w in range(4):
         finish(b_steps(w, None))
         for k in range(BC):
             finish(b_steps(w, k))
+    loop(lambda j: send_out(j).wait())
 
 
 def local(p_blocks, p_rows, c_rows):
     blocks = p_blocks.reshape(SLOTS * NCOL, BLK, BLK)
-    rows, targets = p_rows[0], c_rows[0]
+    rows, targets = p_rows.transpose(1, 0, 2), c_rows.transpose(1, 0, 2)
     dma = pltpu.SemaphoreType.DMA
     out = pl.pallas_call(
         kernel,
         out_shape=jax.ShapeDtypeStruct((SLOTS, NCOL, BLK, BLK), jnp.float32),
         in_specs=[
             pl.BlockSpec(memory_space=pl.ANY),
-            pl.BlockSpec(memory_space=pltpu.SMEM),
-            pl.BlockSpec(memory_space=pltpu.SMEM),
-            pl.BlockSpec(memory_space=pltpu.VMEM),
+            pl.BlockSpec(memory_space=pl.ANY),
+            pl.BlockSpec(memory_space=pl.ANY),
         ],
-        out_specs=pl.BlockSpec(memory_space=pltpu.VMEM),
+        out_specs=pl.BlockSpec(memory_space=pl.ANY),
         scratch_shapes=[pltpu.VMEM((NA + 1, BLK, BLK), jnp.bfloat16)] * 4
         + [pltpu.SMEM((8, 128), jnp.int32)] * 4
         + [
@@ -371,12 +484,18 @@
             dma((4,)), dma((3, 4)), dma((4,)),
             dma((4, BC)), dma((3, 4, BC)), dma((4,)), dma((3, 4)),
             dma((4,)), dma,
+            pltpu.SMEM((SLOTS, 1, NCOL), jnp.int32),
+            pltpu.SMEM((SLOTS, 1, NCOL), jnp.int32),
+            pltpu.VMEM((SLOTS, 1, NCOL), jnp.int32),
+            dma((3,)),
+            pltpu.VMEM((SLOTS, NCOL, BLK, BLK), jnp.float32),
+            dma((NCOL,)),
         ],
         compiler_params=pltpu.CompilerParams(
-            collective_id=0, has_side_effects=True, vmem_limit_bytes=32 * 1024 * 1024
+            collective_id=0, has_side_effects=True, vmem_limit_bytes=60 * 1024 * 1024
         ),
         name="panels",
-    )(blocks, rows, targets, rows)
+    )(blocks, rows, targets)
     return out[None]
 
 

time: 48.4 us -> 43.4 us (0.90)
  the two profiles are of different devices: /device:TPU:8 before, /device:TPU:1 now
where the time goes in v2:
time: 43.4 us; the launch traced here: 43.3 us
  Pallas kernels  40.6 us (94%)
  local copies, waits for them, and re-layouts  2.7 us (6%)
    pallas_call x1, Pallas kernels, local(): pl.pallas_call(kernel, out_shape=jax.ShapeDtypeStruct((SLOTS, NCOL, BLK,...  40.6 us
    unnamed x1, local copies, waits for them, and re-layouts  2.7 us

profile of v2, /device:TPU:1, one launch (start us, length us, event | category | flops | bytes accessed | tf_op | source)
XLA Modules:
  0.0 43.3 jit_solution(8379869324951435674)
XLA Ops:
  0.0 40.6 %panels.1 = f32[3,8,128,128]{3,2,1,0:T(8,128)} custom-call(bf16[24,128,128]{2,1,0:T(8,128)(2,1)} %bitcast.5, s32[3,1,8]{2,1,0:T(1,128)} %bitcast.6, s32[3,1,8]{2,1,0:T(1,128)} %bitcast.7), custom_call_target="tpu_custom_call" | custom-call | tf_op jit(solution)/shard_map/panels/pallas_call | solution.py:462
  40.6 2.7 %copy.5 = f32[1,3,8,128,128]{4,3,2,1,0:T(8,128)} copy(f32[1,3,8,128,128]{4,3,2,1,0:T(8,128)} %bitcast.4) | data formatting | bytes 3145728

commit v3 on v2

v3 whole, which is shorter than its diff:
```python
import functools

import jax
import jax.numpy as jnp
from jax import lax
from jax.experimental import pallas as pl
from jax.experimental.pallas import tpu as pltpu
from jax.sharding import PartitionSpec as P

MESH = pl.DeviceIdType.MESH
BLK = 128
NCOL = 8
SLOTS = 3
NA = 16
NB = 6
HALF = NA // 2
AC = 8
AB = HALF // AC
EARLY = AC // 2
BC = 2
BB = NB // BC
RX, RZ = 4, 8


def kernel(p_hbm, rows_hbm, targets_hbm, acc, *scratch):
    a_bufs = scratch[0:4]
    tab_s = scratch[4:8]
    (b_buf, tab_v, bm_v, bm_s, p_v, ids, a_pick, b_pick, p_sem,
     a_recv, a_srecv, a_ssend, a_send, t_recv, t_send, t_sib,
     b_recv, b_send, m_recv, m_send, loc_sem, bm_sem, rows_s, targets_s, rows_v, in_sem, chain) = scratch[8:]

    r, c = lax.axis_index("row"), lax.axis_index("col")
    x, y_lo = r % RX, r // RX
    core, z, y_hi = c % 2, (c // 2) % RZ, c // (2 * RZ)

    def device(x, y_lo, y_hi, z, core):
        return (y_lo * RX + x, (y_hi * RZ + z) * 2 + core)

    z_up = device(x, y_lo, y_hi, (z + 1) % RZ, core)
    z_down = device(x, y_lo, y_hi, (z + RZ - 1) % RZ, core)
    y_far = device(x, y_lo, 1 - y_hi, z, core)
    sib = device(x, y_lo, y_hi, z, 1 - core)
    x_up = device((x + 1) % RX, y_lo, y_hi, z, core)
    x_down = device((x + RX - 1) % RX, y_lo, y_hi, z, core)
    x_far = device((x + RX // 2) % RX, y_lo, y_hi, z, core)
    y_near = device(x, 1 - y_lo, y_hi, z, core)
    partners = (z_up, z_down, y_far, sib, x_up, x_down, x_far, y_near)

    barrier = pltpu.get_barrier_semaphore()
    for partner in partners:
        pl.semaphore_signal(barrier, inc=1, device_id=partner, device_id_type=MESH)

    row_copy = pltpu.make_async_copy(rows_hbm, rows_s, in_sem.at[0])
    row_copy_v = pltpu.make_async_copy(rows_hbm, rows_v, in_sem.at[1])
    target_copy = pltpu.make_async_copy(targets_hbm, targets_s, in_sem.at[2])
    a_root = (z % (RZ // 2) == 0) & (core == 0)
    b_root = x % (RX // 2) == 0
    fetch = pltpu.make_async_copy(p_hbm, p_v, p_sem)

    @pl.when(a_root | b_root)
    def _():
        row_copy.start()
        row_copy_v.start()
        fetch.start()

    target_copy.start()

    for u in range(4):
        a_bufs[u][NA] = jnp.zeros((BLK, BLK), jnp.bfloat16)

    lane = lax.broadcasted_iota(jnp.int32, (8, 128), 1)
    sub = lax.broadcasted_iota(jnp.int32, (8, 128), 0)

    def pick(stored, slots, out):
        last = SLOTS * NCOL - 1
        here = jnp.int32(last)
        chain[last + 1] = here
        for f in range(last, -1, -1):
            here = jnp.where(stored(rows_s[f // NCOL, 0, f % NCOL]), f, here)
            chain[f] = here
        place = chain[0]
        out[0] = place
        for i in range(1, slots):
            place = chain[place + 1]
            out[i] = place

    def before(ones):
        return prefix(ones) - ones

    def row_sum(ones):
        return jnp.sum(ones, axis=1, keepdims=True)

    def prefix(ones):
        total = ones + pltpu.roll(ones, 1, 1)
        total = total + pltpu.roll(total, 2, 1)
        return total + pltpu.roll(total, 4, 1)

    def is_a(row):
        return row >= 0

    def is_b(row):
        return (row >= 0) & (row < NCOL)

    @pl.when(a_root | b_root)
    def _():
        row_copy.wait()

    @pl.when(a_root)
    def _():
        pick(is_a, NA, a_pick)

    @pl.when(b_root)
    def _():
        pick(is_b, NB, b_pick)

    def load_ids():
        row_copy_v.wait()
        ids[...] = jnp.full((8, 128), -1, jnp.int32)
        for e in range(SLOTS):
            ids[e:e + 1, 0:NCOL] = rows_v[e]

    def b_table():
        held = ids[...]
        live = is_b(held)
        ones = jnp.where(live, 1, 0)
        sums = row_sum(ones)
        base = jnp.where(sub >= 1, sums[0:1], 0) + jnp.where(sub >= 2, sums[1:2], 0)
        v = x // (RX // 2)
        bm_v[v, 0] = jnp.where(live, held, NCOL)
        bm_v[v, 1] = jnp.where(live, jnp.minimum(before(ones) + base, NB - 1), 0)

    def a_table():
        table = jnp.full((8, 128), NA, jnp.int32)
        wanted = lane // 32 * 8 + sub
        base = jnp.zeros((8, 1), jnp.int32)
        for e in range(SLOTS):
            one = jnp.broadcast_to(ids[e:e + 1, :], (8, 128))
            two = jnp.maximum(one, pltpu.roll(one, 32, 1))
            four = jnp.maximum(two, pltpu.roll(two, 64, 1))
            ones = jnp.where(is_a(four), 1, 0)
            table = jnp.where(four == wanted, jnp.minimum(before(ones) + base, NA), table)
            base = base + row_sum(ones) // 4
        tab_v[z // (RZ // 2)] = table

    @pl.when(a_root | b_root)
    def _():
        fetch.wait()

    @pl.when(b_root)
    def _():
        for i in range(NB):
            b_buf[x // (RX // 2), i] = p_v[b_pick[i]]

    for v in range(2):
        @pl.when(a_root & (z == v * (RZ // 2)))
        def _(v=v):
            for i in range(NA):
                a_bufs[v][i] = p_v[a_pick[i]]

    pl.semaphore_wait(barrier, len(partners))

    def remote(src, dst, send, recv, to):
        return pltpu.make_async_remote_copy(
            src_ref=src, dst_ref=dst, send_sem=send, recv_sem=recv, device_id=to, device_id_type=MESH
        )

    def a_steps(u, k):
        flag, v = divmod(u, 2)
        d = (z + RZ - v * (RZ // 2)) % RZ
        mine = pl.ds(core * HALF + k * AB, AB)
        other = pl.ds((1 - core) * HALF + k * AB, AB)
        part, far = a_bufs[u].at[mine], a_bufs[u].at[other]
        even = k % 2 == 0
        up = (d <= 2) | ((d == 3) & even)
        down = (d == 0) | (d >= 6) | ((d == 5) & (k % 2 == 1))
        if flag:
            up, down = up & (k >= EARLY), down & (k >= EARLY)
        out = dict(
            up=(up, remote(part, part, a_send.at[0, u, k], a_recv.at[u, k], z_up)),
            down=(down, remote(part, part, a_send.at[1, u, k], a_recv.at[u, k], z_down)),
            side=(None, remote(part, part, a_ssend.at[u, k], a_srecv.at[u, k], sib)),
        )
        if flag == 0:
            across = a_bufs[u + 2].at[mine]
            out["side"] = ((d != 0) | (core == 0), out["side"][1])
            out["across"] = (
                (d == 0) | (k < EARLY), remote(part, across, a_send.at[2, u, k], a_recv.at[u + 2, k], y_far)
            )
            out["far"] = (
                (d == 0) & (core == 0), remote(far, far, a_ssend.at[u, AC + k], a_recv.at[u, k], sib)
            )
        return out

    def t_steps(u):
        flag, v = divmod(u, 2)
        d = (z + RZ - v * (RZ // 2)) % RZ
        part = tab_v.at[u]
        out = []
        if flag == 0:
            root = (d == 0) & (core == 0)
            out.append((root, remote(part, part, t_sib.at[u], t_recv.at[u], sib)))
        out.append((d <= 3, remote(part, part, t_send.at[0, u], t_recv.at[u], z_up)))
        out.append(((d == 0) | (d >= 6), remote(part, part, t_send.at[1, u], t_recv.at[u], z_down)))
        if flag == 0:
            out.append((d == 0, remote(part, tab_v.at[u + 2], t_send.at[2, u], t_recv.at[u + 2], y_far)))
        return out

    def b_steps(w, k):
        flag, v = divmod(w, 2)
        d = (x + RX - v * (RX // 2)) % RX
        if k is None:
            part, across = bm_v.at[w], bm_v.at[w % 2 + 2]
            send = lambda n: m_send.at[n, w]
            recv = lambda w: m_recv.at[w]
        else:
            part, across = b_buf.at[w, pl.ds(k * BB, BB)], b_buf.at[w % 2 + 2, pl.ds(k * BB, BB)]
            send = lambda n: b_send.at[n, w, k]
            recv = lambda w: b_recv.at[w, k]
        out = []
        if flag == 0:
            out.append((d == 0, remote(part, across, send(3), recv(w + 2), y_near)))
        for n, to in enumerate((x_up, x_down, x_far)):
            out.append((d == 0, remote(part, part, send(n), recv(w), to)))
        return out

    def start(steps):
        for condition, copy in steps:
            if condition is None:
                copy.start()
            else:
                pl.when(condition)(copy.start)

    def finish(steps):
        for condition, copy in steps:
            if condition is None:
                copy.wait_send()
            else:
                pl.when(condition)(copy.wait_send)

    def arrived(buf, sem):
        remote(buf, buf, loc_sem.at[0], sem, sib).wait_recv()

    def loop(body, low=0, high=AC):
        def step(k, _):
            body(k)
            return 0

        lax.fori_loop(low, high, step, 0)

    def mine(u, k):
        return a_bufs[u].at[pl.ds(core * HALF + k * AB, AB)]

    def relay_a(u, k):
        arrived(mine(u, k), a_recv.at[u, k])
        steps = a_steps(u, k)
        steps.pop("far", None)
        start(steps.values())

    def order(i, side):
        base = i // 4 * 4 + i % 2 * 2 + i // 2 % 2
        return base + side * (1 - 2 * (base % 2))

    def side_of(u):
        return ((z + RZ - u % 2 * (RZ // 2)) % RZ + 3) // RZ

    def relay_range(u, low, high):
        side = side_of(u)
        loop(lambda i: relay_a(u, order(i, side)), low, high)

    def at_root(u):
        return z == u * (RZ // 2)

    def relay_own(u, between=None):
        @pl.when(~at_root(u))
        def _():
            if between is None:
                relay_range(u, 0, 6)
            else:
                relay_range(u, 0, 3)
                between()
                relay_range(u, 3, 6)

        @pl.when(at_root(u))
        def _():
            @pl.when(core == 0)
            def _():
                loop(lambda k: a_steps(u, k)["far"][1].start())

            @pl.when(core == 1)
            def _():
                loop(lambda k: arrived(mine(u, k), a_recv.at[u, k]))

            def send(i):
                a_steps(u, order(i, 0))["up"][1].start()
                a_steps(u, order(i, 1))["down"][1].start()

            def send_across(i):
                send(i)
                a_steps(u, order(i + EARLY, 0))["across"][1].start()

            loop(send_across, 0, EARLY)
            loop(send, EARLY, 6)
            loop(lambda k: start([a_steps(u, k)["side"]]))

    def relay_own_late(u):
        @pl.when(~at_root(u))
        def _():
            relay_range(u, 6, 8)

        @pl.when(at_root(u))
        def _():
            def send(i):
                a_steps(u, order(i, 0))["up"][1].start()
                a_steps(u, order(i, 1))["down"][1].start()

            loop(send, 6)
            loop(lambda i: a_steps(u, order(i, 0))["across"][1].start(), 0, EARLY)

    def relay_late(u):
        relay_range(u, EARLY, AC)

    def relay_early(u):
        relay_range(u, 0, EARLY)

    def relay_t(u):
        flag, v = divmod(u, 2)
        if flag == 0:
            @pl.when((z != v * (RZ // 2)) | (core != 0))
            def _():
                arrived(tab_v.at[u], t_recv.at[u])
        else:
            arrived(tab_v.at[u], t_recv.at[u])
        start(t_steps(u))
        pltpu.make_async_copy(tab_v.at[u], tab_s[u], loc_sem.at[u]).start()

    def b_wait(w):
        arrived(bm_v.at[w], m_recv.at[w])
        for k in range(BC):
            arrived(b_buf.at[w, pl.ds(k * BB, BB)], b_recv.at[w, k])

    def b_distance(w):
        return (x + RX - (w % 2) * (RX // 2)) % RX

    def send_b(w):
        @pl.when(b_distance(w) == 0)
        def _():
            for k in range(BC):
                if w >= 2:
                    arrived(b_buf.at[w, pl.ds(k * BB, BB)], b_recv.at[w, k])
                start(b_steps(w, k))
            if w >= 2:
                arrived(bm_v.at[w], m_recv.at[w])
                start(b_steps(w, None))

    for w in (0, 1):
        send_b(w)

    def b_own_tables():
        @pl.when(b_root)
        def _():
            b_table()
            for w in (0, 1):
                pl.when(b_distance(w) == 0)(lambda w=w: start(b_steps(w, None)))

    def b_peers():
        for w in (2, 3):
            send_b(w)

    def b_ready():
        for w in range(4):
            pl.when(b_distance(w) != 0)(functools.partial(b_wait, w))
        to_smem = pltpu.make_async_copy(bm_v, bm_s, bm_sem)
        to_smem.start()
        to_smem.wait()

    def a_ready(u):
        pltpu.make_async_copy(tab_v.at[u], tab_s[u], loc_sem.at[u]).wait()

        def wait(k):
            arrived(a_bufs[u].at[pl.ds((1 - core) * HALF + k * AB, AB)], a_srecv.at[u, k])

        if u < 2:
            @pl.when((z != u * (RZ // 2)) | (core != 0))
            def _():
                loop(wait)
        else:
            loop(wait)

    def column(pair, j, first):
        places = []
        for s in range(SLOTS):
            target = targets_s[s, 0, j]
            places.append((target % 8, target // 8 * 32))
        left, right = [], []
        for u in pair:
            flag, v = divmod(u, 2)
            w = (flag + y_hi + y_lo) % 2 * 2 + v
            panel, table = a_bufs[u], tab_s[u]
            for e in range(SLOTS):
                at = bm_s[w, 0, e, j]
                right.append(b_buf[w, bm_s[w, 1, e, j]])
                left.append([panel[table[low, high + at]] for low, high in places])
        right = jnp.concatenate(right, axis=0)
        for s in range(SLOTS):
            piece = jnp.dot(
                jnp.concatenate([blocks[s] for blocks in left], axis=1), right, preferred_element_type=jnp.float32
            )
            acc[s, j] = piece if first else acc[s, j] + piece

    target_copy.wait()
    def columns(pair, first):
        def step(i):
            for j in (i * 2, i * 2 + 1):
                column(pair, j, first)

        loop(step, 0, NCOL // 2)

    for near in (0, 1):
        @pl.when((z % 4 != 2) & ((z + 2) // 4 % 2 == near))
        def _(near=near):
            far = 1 - near
            relay_own(near)
            pl.when(a_root | b_root)(load_ids)
            pl.when(a_root)(a_table)
            relay_t(near)
            b_own_tables()
            pl.when(z % 4 != 0)(b_peers)
            relay_late(near + 2)
            relay_t(near + 2)
            relay_own_late(near)
            pl.when(z % 4 == 0)(b_peers)
            relay_early(near + 2)
            relay_own(far)
            relay_t(far)

            @pl.when(z % 4 == 0)
            def _():
                relay_own_late(far)

            @pl.when(z % 4 != 0)
            def _():
                relay_late(far + 2)
                relay_t(far + 2)

            b_ready()
            a_ready(near)
            a_ready(near + 2)

            @pl.when(z % 4 == 0)
            def _():
                def step(i):
                    column((near, near + 2), i * 2, True)
                    column((near, near + 2), i * 2 + 1, True)
                    relay_a(far + 2, order(i + EARLY, side_of(far)))

                loop(step, 0, EARLY)
                relay_t(far + 2)
                relay_early(far + 2)

            @pl.when(z % 4 != 0)
            def _():
                def step(i):
                    relay_a(far + 2, order(i, side_of(far)))

                    @pl.when(i >= 2)
                    def _():
                        relay_a(far, order(i + EARLY, side_of(far)))

                    column((near, near + 2), i * 2, True)
                    column((near, near + 2), i * 2 + 1, True)

                loop(step, 0, EARLY)

            a_ready(far)
            a_ready(far + 2)

            columns((far, far + 2), False)

    @pl.when(z % 4 == 2)
    def _():
        @pl.when(b_root)
        def _():
            load_ids()

        b_own_tables()

        def both(u, low, high):
            def step(i):
                relay_a(u, order(i, side_of(0)))
                relay_a(u + 1, order(i, side_of(1)))

            loop(step, low, high)

        both(0, 0, 3)
        b_peers()
        both(0, 3, 6)
        relay_t(0)
        relay_t(1)
        both(2, EARLY, AC)
        relay_t(2)
        relay_t(3)
        both(0, 6, AC)
        both(2, 0, EARLY)
        b_ready()
        a_ready(0)
        a_ready(2)
        columns((0, 2), True)
        a_ready(1)
        a_ready(3)

        columns((1, 3), False)

    for u in range(4):
        finish(t_steps(u))
        loop(lambda k: finish(a_steps(u, k).values()))
    for w in range(4):
        finish(b_steps(w, None))
        for k in range(BC):
            finish(b_steps(w, k))


def local(p_blocks, p_rows, c_rows):
    blocks = p_blocks.reshape(SLOTS * NCOL, BLK, BLK)
    rows, targets = p_rows.transpose(1, 0, 2), c_rows.transpose(1, 0, 2)
    dma = pltpu.SemaphoreType.DMA
    out = pl.pallas_call(
        kernel,
        out_shape=pltpu.VMEM((SLOTS, NCOL, BLK, BLK), jnp.float32),
        in_specs=[
            pl.BlockSpec(memory_space=pl.ANY),
            pl.BlockSpec(memory_space=pl.ANY),
            pl.BlockSpec(memory_space=pl.ANY),
        ],
        out_specs=pl.BlockSpec(memory_space=pltpu.VMEM),
        scratch_shapes=[pltpu.VMEM((NA + 1, BLK, BLK), jnp.bfloat16)] * 4
        + [pltpu.SMEM((8, 128), jnp.int32)] * 4
        + [
            pltpu.VMEM((4, NB, BLK, BLK), jnp.bfloat16),
            pltpu.VMEM((4, 8, 128), jnp.int32),
            pltpu.VMEM((4, 2, 8, 128), jnp.int32),
            pltpu.SMEM((4, 2, 8, 128), jnp.int32),
            pltpu.VMEM((SLOTS * NCOL, BLK, BLK), jnp.bfloat16),
            pltpu.VMEM((8, 128), jnp.int32),
            pltpu.SMEM((NA,), jnp.int32),
            pltpu.SMEM((NB,), jnp.int32),
            dma,
            dma((4, AC)), dma((4, AC)), dma((4, 2 * AC)), dma((3, 4, AC)),
            dma((4,)), dma((3, 4)), dma((4,)),
            dma((4, BC)), dma((4, 4, BC)), dma((4,)), dma((4, 4)),
            dma((4,)), dma,
            pltpu.SMEM((SLOTS, 1, NCOL), jnp.int32),
            pltpu.SMEM((SLOTS, 1, NCOL), jnp.int32),
            pltpu.VMEM((SLOTS, 1, NCOL), jnp.int32),
            dma((3,)),
            pltpu.SMEM((SLOTS * NCOL + 1,), jnp.int32),
        ],
        compiler_params=pltpu.CompilerParams(
            collective_id=0, has_side_effects=True, vmem_limit_bytes=(65536 - 4096) * 1024
        ),
        name="panels",
    )(blocks, rows, targets)
    return out[None]


def solution(mesh):
    placed = (P("row", None, "col", None, None), P("row", None, "col"), P("row", None, "col"))
    return jax.shard_map(
        local,
        mesh=mesh,
        in_specs=placed,
        out_specs=P("row", None, "col", None, None),
        check_vma=False,
    )
```

time: 43.4 us -> 40.6 us (0.935)
  local copies, waits for them, and re-layouts: 2.7 us -> 1.15 us
  Pallas kernels: 40.6 us -> 39.4 us
    unnamed x1, local copies, waits for them, and re-layouts: 2.7 us -> 1.15 us
    pallas_call x1, Pallas kernels: 40.6 us -> 39.4 us  [local(): pl.pallas_call(kernel, out_shape=pltpu.VMEM((SLOTS, NCOL, BLK, BLK), jnp....]
where the time goes in v3:
time: 40.6 us; the launch traced here: 40.5 us
  Pallas kernels  39.4 us (97%)
  local copies, waits for them, and re-layouts  1.15 us (3%)
    pallas_call x1, Pallas kernels, local(): pl.pallas_call(kernel, out_shape=pltpu.VMEM((SLOTS, NCOL, BLK, BLK), jnp....  39.4 us
    unnamed x1, local copies, waits for them, and re-layouts  1.15 us

profile of v3, /device:TPU:1, one launch (start us, length us, event | category | flops | bytes accessed | tf_op | source)
XLA Modules:
  0.0 40.5 jit_solution(3924277566619499652)
XLA Ops:
  0.0 39.4 %panels.1 = f32[3,8,128,128]{3,2,1,0:T(8,128)S(1)} custom-call(bf16[24,128,128]{2,1,0:T(8,128)(2,1)} %bitcast.5, s32[3,1,8]{2,1,0:T(1,128)} %bitcast.6, s32[3,1,8]{2,1,0:T(1,128)} %bitcast.7), custom_call_target="tpu_custom_call" | custom-call | tf_op jit(solution)/shard_map/panels/pallas_call | solution.py:526
  39.4 1.1 %copy.5 = f32[1,3,8,128,128]{4,3,2,1,0:T(8,128)} copy(f32[1,3,8,128,128]{4,3,2,1,0:T(8,128)S(1)} %bitcast.4) | data formatting | bytes 3145728

commit v4 on v3

--- a/solution.py
+++ b/solution.py
@@ -109,10 +109,6 @@
     def _():
         pick(is_a, NA, a_pick)
 
-    @pl.when(b_root)
-    def _():
-        pick(is_b, NB, b_pick)
-
     def load_ids():
         row_copy_v.wait()
         ids[...] = jnp.full((8, 128), -1, jnp.int32)
@@ -145,11 +141,6 @@
     @pl.when(a_root | b_root)
     def _():
         fetch.wait()
-
-    @pl.when(b_root)
-    def _():
-        for i in range(NB):
-            b_buf[x // (RX // 2), i] = p_v[b_pick[i]]
 
     for v in range(2):
         @pl.when(a_root & (z == v * (RZ // 2)))
@@ -218,9 +209,10 @@
             recv = lambda w: b_recv.at[w, k]
         out = []
         if flag == 0:
-            out.append((d == 0, remote(part, across, send(3), recv(w + 2), y_near)))
+            out.append((d != 2 if k == 0 else d == 0, remote(part, across, send(3), recv(w + 2), y_near)))
         for n, to in enumerate((x_up, x_down, x_far)):
-            out.append((d == 0, remote(part, part, send(n), recv(w), to)))
+            if n == 2 or flag == 0 or k != 0:
+                out.append((d == 0, remote(part, part, send(n), recv(w), to)))
         return out
 
     def start(steps):
@@ -336,7 +328,13 @@
     def b_wait(w):
         arrived(bm_v.at[w], m_recv.at[w])
         for k in range(BC):
-            arrived(b_buf.at[w, pl.ds(k * BB, BB)], b_recv.at[w, k])
+            def wait(k=k):
+                arrived(b_buf.at[w, pl.ds(k * BB, BB)], b_recv.at[w, k])
+
+            if w < 2 and k == 0:
+                pl.when(b_distance(w) == 2)(wait)
+            else:
+                wait()
 
     def b_distance(w):
         return (x + RX - (w % 2) * (RX // 2)) % RX
@@ -347,13 +345,24 @@
             for k in range(BC):
                 if w >= 2:
                     arrived(b_buf.at[w, pl.ds(k * BB, BB)], b_recv.at[w, k])
-                start(b_steps(w, k))
+                start(b_steps(w, k)[:-1])
+            for k in range(BC):
+                start(b_steps(w, k)[-1:])
             if w >= 2:
                 arrived(bm_v.at[w], m_recv.at[w])
                 start(b_steps(w, None))
 
-    for w in (0, 1):
-        send_b(w)
+    def b_begin():
+        @pl.when(b_root)
+        def _():
+            pick(is_b, NB, b_pick)
+            for i in range(NB):
+                b_buf[x // (RX // 2), i] = p_v[b_pick[i]]
+
+        for w in (0, 1):
+            send_b(w)
+
+    pl.when(~a_root)(b_begin)
 
     def b_own_tables():
         @pl.when(b_root)
@@ -363,6 +372,12 @@
                 pl.when(b_distance(w) == 0)(lambda w=w: start(b_steps(w, None)))
 
     def b_peers():
+        for w in (0, 1):
+            @pl.when(b_distance(w) % 2 == 1)
+            def _(w=w):
+                arrived(b_buf.at[w, pl.ds(0, BB)], b_recv.at[w, 0])
+                start(b_steps(w, 0)[:1])
+
         for w in (2, 3):
             send_b(w)
 
@@ -420,6 +435,7 @@
         def _(near=near):
             far = 1 - near
             relay_own(near)
+            pl.when(a_root)(b_begin)
             pl.when(a_root | b_root)(load_ids)
             pl.when(a_root)(a_table)
             relay_t(near)

time: 40.6 us -> 38.5 us (0.948)
  Pallas kernels: 39.4 us -> 37.3 us
    pallas_call x1, Pallas kernels: 39.4 us -> 37.3 us  [local(): pl.pallas_call(kernel, out_shape=pltpu.VMEM((SLOTS, NCOL, BLK, BLK), jnp....]
where the time goes in v4:
time: 38.5 us; the launch traced here: 38.4 us
  Pallas kernels  37.3 us (97%)
  local copies, waits for them, and re-layouts  1.15 us (3%)
    pallas_call x1, Pallas kernels, local(): pl.pallas_call(kernel, out_shape=pltpu.VMEM((SLOTS, NCOL, BLK, BLK), jnp....  37.3 us
    unnamed x1, local copies, waits for them, and re-layouts  1.15 us

profile of v4, /device:TPU:1, one launch (start us, length us, event | category | flops | bytes accessed | tf_op | source)
XLA Modules:
  0.0 38.4 jit_solution(12383035088965610886)
XLA Ops:
  0.0 37.3 %panels.1 = f32[3,8,128,128]{3,2,1,0:T(8,128)S(1)} custom-call(bf16[24,128,128]{2,1,0:T(8,128)(2,1)} %bitcast.5, s32[3,1,8]{2,1,0:T(1,128)} %bitcast.6, s32[3,1,8]{2,1,0:T(1,128)} %bitcast.7), custom_call_target="tpu_custom_call" | custom-call | tf_op jit(solution)/shard_map/panels/pallas_call | solution.py:542
  37.3 1.1 %copy.5 = f32[1,3,8,128,128]{4,3,2,1,0:T(8,128)} copy(f32[1,3,8,128,128]{4,3,2,1,0:T(8,128)S(1)} %bitcast.4) | data formatting | bytes 3145728

commit v5 on v4

--- a/solution.py
+++ b/solution.py
@@ -46,10 +46,6 @@
     y_near = device(x, 1 - y_lo, y_hi, z, core)
     partners = (z_up, z_down, y_far, sib, x_up, x_down, x_far, y_near)
 
-    barrier = pltpu.get_barrier_semaphore()
-    for partner in partners:
-        pl.semaphore_signal(barrier, inc=1, device_id=partner, device_id_type=MESH)
-
     row_copy = pltpu.make_async_copy(rows_hbm, rows_s, in_sem.at[0])
     row_copy_v = pltpu.make_async_copy(rows_hbm, rows_v, in_sem.at[1])
     target_copy = pltpu.make_async_copy(targets_hbm, targets_s, in_sem.at[2])
@@ -64,6 +60,10 @@
         fetch.start()
 
     target_copy.start()
+
+    barrier = pltpu.get_barrier_semaphore()
+    for partner in partners:
+        pl.semaphore_signal(barrier, inc=1, device_id=partner, device_id_type=MESH)
 
     for u in range(4):
         a_bufs[u][NA] = jnp.zeros((BLK, BLK), jnp.bfloat16)
@@ -276,21 +276,24 @@
         def _():
             @pl.when(core == 0)
             def _():
-                loop(lambda k: a_steps(u, k)["far"][1].start())
-
-            @pl.when(core == 1)
-            def _():
-                loop(lambda k: arrived(mine(u, k), a_recv.at[u, k]))
+                for k in (0, 1, 4, 2, 3, 6, 5, 7):
+                    a_steps(u, k)["far"][1].start()
 
             def send(i):
                 a_steps(u, order(i, 0))["up"][1].start()
                 a_steps(u, order(i, 1))["down"][1].start()
 
             def send_across(i):
+                @pl.when(core == 1)
+                def _():
+                    for k in ((0, 1, 4), (2, 3, 6), (5,), (7,))[i]:
+                        arrived(mine(u, k), a_recv.at[u, k])
+
                 send(i)
                 a_steps(u, order(i + EARLY, 0))["across"][1].start()
 
-            loop(send_across, 0, EARLY)
+            for i in range(EARLY):
+                send_across(i)
             loop(send, EARLY, 6)
             loop(lambda k: start([a_steps(u, k)["side"]]))
 
@@ -423,6 +426,10 @@
             acc[s, j] = piece if first else acc[s, j] + piece
 
     target_copy.wait()
+    def a_sent(u):
+        finish(t_steps(u))
+        loop(lambda k: finish(a_steps(u, k).values()))
+
     def columns(pair, first):
         def step(i):
             for j in (i * 2, i * 2 + 1):
@@ -458,6 +465,8 @@
                 relay_late(far + 2)
                 relay_t(far + 2)
 
+            a_sent(near)
+            a_sent(near + 2)
             b_ready()
             a_ready(near)
             a_ready(near + 2)
@@ -491,6 +500,8 @@
             a_ready(far + 2)
 
             columns((far, far + 2), False)
+            a_sent(far)
+            a_sent(far + 2)
 
     @pl.when(z % 4 == 2)
     def _():
@@ -517,6 +528,8 @@
         relay_t(3)
         both(0, 6, AC)
         both(2, 0, EARLY)
+        for u in range(4):
+            a_sent(u)
         b_ready()
         a_ready(0)
         a_ready(2)
@@ -526,9 +539,6 @@
 
         columns((1, 3), False)
 
-    for u in range(4):
-        finish(t_steps(u))
-        loop(lambda k: finish(a_steps(u, k).values()))
     for w in range(4):
         finish(b_steps(w, None))
         for k in range(BC):

time: 38.5 us -> 38.3 us (level)
  no operation moved by 1% of the time
where the time goes in v5:
time: 38.3 us; the launch traced here: 38.2 us
  Pallas kernels  37.1 us (97%)
  local copies, waits for them, and re-layouts  1.15 us (3%)
    pallas_call x1, Pallas kernels, local(): pl.pallas_call(kernel, out_shape=pltpu.VMEM((SLOTS, NCOL, BLK, BLK), jnp....  37.1 us
    unnamed x1, local copies, waits for them, and re-layouts  1.15 us

profile of v5, /device:TPU:1, one launch (start us, length us, event | category | flops | bytes accessed | tf_op | source)
XLA Modules:
  0.0 38.2 jit_solution(10228668635603753400)
XLA Ops:
  0.0 37.1 %panels.1 = f32[3,8,128,128]{3,2,1,0:T(8,128)S(1)} custom-call(bf16[24,128,128]{2,1,0:T(8,128)(2,1)} %bitcast.5, s32[3,1,8]{2,1,0:T(1,128)} %bitcast.6, s32[3,1,8]{2,1,0:T(1,128)} %bitcast.7), custom_call_target="tpu_custom_call" | custom-call | tf_op jit(solution)/shard_map/panels/pallas_call | solution.py:552
  37.1 1.1 %copy.5 = f32[1,3,8,128,128]{4,3,2,1,0:T(8,128)} copy(f32[1,3,8,128,128]{4,3,2,1,0:T(8,128)S(1)} %bitcast.4) | data formatting | bytes 3145728

commit v6 on v4

--- a/solution.py
+++ b/solution.py
@@ -425,10 +425,10 @@
     target_copy.wait()
     def columns(pair, first):
         def step(i):
-            for j in (i * 2, i * 2 + 1):
-                column(pair, j, first)
-
-        loop(step, 0, NCOL // 2)
+            for part in range(4):
+                column(pair, i * 4 + part, first)
+
+        loop(step, 0, NCOL // 4)
 
     for near in (0, 1):
         @pl.when((z % 4 != 2) & ((z + 2) // 4 % 2 == near))

time: 38.5 us -> 38.2 us (level)
  Pallas kernels: 37.3 us -> 36.9 us
where the time goes in v6:
time: 38.2 us; the launch traced here: 38.1 us
  Pallas kernels  36.9 us (97%)
  local copies, waits for them, and re-layouts  1.15 us (3%)
    pallas_call x1, Pallas kernels, local(): pl.pallas_call(kernel, out_shape=pltpu.VMEM((SLOTS, NCOL, BLK, BLK), jnp....  36.9 us
    unnamed x1, local copies, waits for them, and re-layouts  1.15 us

profile of v6, /device:TPU:1, one launch (start us, length us, event | category | flops | bytes accessed | tf_op | source)
XLA Modules:
  0.0 38.1 jit_solution(5719843216886757509)
XLA Ops:
  0.0 36.9 %panels.1 = f32[3,8,128,128]{3,2,1,0:T(8,128)S(1)} custom-call(bf16[24,128,128]{2,1,0:T(8,128)(2,1)} %bitcast.5, s32[3,1,8]{2,1,0:T(1,128)} %bitcast.6, s32[3,1,8]{2,1,0:T(1,128)} %bitcast.7), custom_call_target="tpu_custom_call" | custom-call | tf_op jit(solution)/shard_map/panels/pallas_call | solution.py:542
  36.9 1.1 %copy.5 = f32[1,3,8,128,128]{4,3,2,1,0:T(8,128)} copy(f32[1,3,8,128,128]{4,3,2,1,0:T(8,128)S(1)} %bitcast.4) | data formatting | bytes 3145728
